TPU v7x, 1024 devices: a whole 8x8x8 slice. The times are simulated.
1024 devices in a mesh: replica: 32 (over z, y_hi, core), fsdp: 8 (over x), tensor: 4 (over y_lo).
Axes of the slice: x: 8, y: 8 (y_hi: 2, y_lo: 4; y = y_hi * 4 + y_lo), z: 8, core: 2. Of those that a mesh axis runs over, the one named last changes fastest.
Arguments:
- layer_input: bfloat16 [32768, 8192], P(('replica', 'fsdp')), may hold values from -6 to 6
- norm_gain: float32 [8192], replicated, may hold values from 0.5 to 1.5
- value_weight: bfloat16 [32, 8192, 1024], P('replica', 'fsdp', 'tensor'), may hold values from -0.0625 to 0.0625
- value_cotangent: bfloat16 [32768, 1024], P(('replica', 'fsdp'), 'tensor'), may hold values from -3 to 3
- token_ids: int32 [32768], P(('replica', 'fsdp')), may hold values from 0 to 128255, as said below
- anchor_weight: float32 [32, 2048, 1024], P('replica', 'fsdp', 'tensor'), may hold values from -0.0625 to 0.0625
- outer_momentum: float32 [32, 2048, 1024], P('replica', 'fsdp', 'tensor'), may hold values from -0.0625 to 0.0625
- gossip_exponent: int32 [4], replicated, may hold values from 0 to 4
- fragment_index: int32 [1], replicated, may hold values from 0 to 3
Outputs:
- value: bfloat16 [32768, 1024], P(('replica', 'fsdp'), 'tensor')
- input_grad: bfloat16 [32768, 8192], P(('replica', 'fsdp'), 'tensor')
- weight_grad: bfloat16 [32, 8192, 1024], P('replica', 'fsdp', 'tensor')
- new_anchor: float32 [32, 2048, 1024], P('replica', 'fsdp', 'tensor')
- new_momentum: float32 [32, 2048, 1024], P('replica', 'fsdp', 'tensor')
- merged_weight: bfloat16 [32, 2048, 1024], P('replica', 'fsdp', 'tensor')
Inputs may be any that keep to these rules, and one draw needn't show every extreme that they name: `token_ids`: some of the ids are the padding id 128004.
All inputs are finite; a program needn't handle non-finite values.
Results may differ from a plain program's by a relative error of at most 0.019.
Values may be sent and summed in bfloat16 or wider, within the bound.
A program may use at most 64 MiB of HBM per device.

v0:
```python
from functools import partial

import jax
import jax.numpy as jnp
from jax import lax
from jax.sharding import PartitionSpec as P

NFRAG = 4
FRAG_ROWS = 256


pad_token = 128004
outer_mu = 0.9
outer_eta = 0.7
merge_alpha = 0.5


def as_sent(value):
    return jax.tree.map(lambda a: a.astype(jnp.bfloat16) if a.dtype == jnp.float32 else a, value)


def swapped(value, axis, bit):
    return lax.ppermute(value, axis, [(i, i ^ 1 << bit) for i in range(lax.axis_size(axis))])


def contract_first(left, right):
    return lax.dot_general(
        left, right, (((0,), (0,)), ((), ())), preferred_element_type=jnp.float32
    )


def contract_last(left, right):
    return lax.dot_general(
        left, right, (((1,), (1,)), ((), ())), preferred_element_type=jnp.float32
    )


def trade(bit, pseudo):
    return jax.tree.map(
        lambda part, own: part.astype(own.dtype), swapped(as_sent(pseudo), "replica", bit), pseudo
    )


def local(
    layer_input,
    norm_gain,
    value_weight,
    value_cotangent,
    token_ids,
    anchor_weight,
    outer_momentum,
    gossip_exponent,
    fragment_index,
):
    xf = layer_input.astype(jnp.float32)
    inv = lax.rsqrt(jnp.mean(xf * xf, axis=1) + 1e-05)
    normed = (xf * inv[:, None] * norm_gain[None, :]).astype(jnp.bfloat16)
    weight = value_weight[0]
    keep = (token_ids != pad_token).astype(jnp.bfloat16)
    cotan = value_cotangent * keep[:, None]
    columns = normed
    value_sum = jnp.dot(
        columns,
        lax.all_gather(weight, "fsdp", axis=0, tiled=True),
        preferred_element_type=jnp.float32,
    )
    partial_rows = contract_last(cotan, lax.all_gather(weight, "fsdp", axis=0, tiled=True)).astype(
        jnp.bfloat16
    )
    grad = lax.psum_scatter(
        contract_first(normed, cotan).astype(jnp.bfloat16), "fsdp", scatter_dimension=0, tiled=True
    )
    value = value_sum.astype(jnp.bfloat16)
    summed = lax.psum_scatter(
        partial_rows.astype(jnp.float32).astype(jnp.bfloat16),
        "tensor",
        scatter_dimension=1,
        tiled=True,
    )
    shard_rows = weight.shape[0]
    columns = weight.shape[1]
    shape4 = (shard_rows // (NFRAG * FRAG_ROWS), NFRAG, FRAG_ROWS, columns)
    index = fragment_index[0]
    weight_f = lax.dynamic_index_in_dim(
        weight.astype(jnp.float32).reshape(shape4), index, 1, keepdims=False
    )
    weight_f = weight_f.reshape(shard_rows // NFRAG, columns)
    anchor_f = anchor_weight[0]
    own = anchor_f - weight_f
    bits = lax.axis_size("replica").bit_length() - 1
    expo = lax.dynamic_index_in_dim(gossip_exponent, index, 0, keepdims=False)
    other = lax.switch(expo, [partial(trade, level) for level in range(bits)], own)
    mean_delta = 0.5 * (own + other)
    momentum_new = outer_mu * outer_momentum[0] + mean_delta
    anchor_new = anchor_f - outer_eta * (mean_delta + outer_mu * momentum_new)
    merged = (merge_alpha * weight_f + (1.0 - merge_alpha) * anchor_new).astype(jnp.bfloat16)
    return (value, summed, grad[None], anchor_new[None], momentum_new[None], merged[None])


def solution(mesh):
    in_specs = (
        P(("replica", "fsdp"), None),
        P(),
        P("replica", "fsdp", "tensor"),
        P(("replica", "fsdp"), "tensor"),
        P(("replica", "fsdp")),
        P("replica", "fsdp", "tensor"),
        P("replica", "fsdp", "tensor"),
        P(),
        P(),
    )
    out_specs = (
        P(("replica", "fsdp"), "tensor"),
        P(("replica", "fsdp"), "tensor"),
        P("replica", "fsdp", "tensor"),
        P("replica", "fsdp", "tensor"),
        P("replica", "fsdp", "tensor"),
        P("replica", "fsdp", "tensor"),
    )
    return jax.shard_map(local, mesh=mesh, in_specs=in_specs, out_specs=out_specs, check_vma=False)
```

profile of v0, /device:TPU:1, one launch (start us, length us, event | category | flops | bytes accessed | tf_op | source)
XLA Modules:
  0.0 211.1 jit_solution(15277800982031541488)
XLA Ops:
  7.2 0.0 all-gather.3.cloned.1.call-start
  7.2 0.7 all-gather.3.cloned.1.call-update
  7.9 0.0 reduce-scatter.5.cloned.1.call-start
  7.9 2.1 fusion
  10.0 0.7 compare_convert_fusion
  10.7 5.0 %convolution_convert_fusion = bf16[8192,256]{1,0:T(8,128)(2,1)} fusion(bf16[128,8192]{1,0:T(8,128)(2,1)} %param.14, f32[8192]{0:T(1024)} %param.15, f32[128]{0:T(128)S(1)} %add_rsqrt_fusion, bf16[128,256]{1,0:T(8,128)(2,1)} %param.17, bf16[128]{0:T(256)(128)(2,1)S(1)} %compare_convert_fusion), kind=kOutput, calls=%fused_computation | convolution fusion | flops 543195136 | bytes 6390528 | tf_op jit(solution)/shard_map/dot_general | solution.py:27
  15.7 0.0 copy-start.3
  15.7 0.0 reduce-scatter.5.cloned.1.call-update
  15.7 0.0 copy-start.5
  15.7 0.0 copy-start.1
  15.8 0.0 copy-start.2
  15.8 0.0 reduce-scatter.3.cloned.1.call-start
  15.8 66.7 %all-gather.3.cloned.1.call-done = bf16[1,8192,256]{2,1,0:T(8,128)(2,1)} async-done(((bf16[1,1024,256]{2,1,0:T(8,128)(2,1)}), bf16[1,8192,256]{2,1,0:T(8,128)(2,1)}) %all-gather.3.cloned.1.call-update) | async-done | bytes 4194320 | tf_op jit(solution)/shard_map/all_gather | solution.py:64
  82.5 0.0 copy-done.3
  82.5 5.0 %convolution_convert_fusion.1 = bf16[128,8192]{1,0:T(8,128)(2,1)} fusion(bf16[1,8192,256]{2,1,0:T(8,128)(2,1)} %all-gather.3.cloned.1.call-done, bf16[128,256]{1,0:T(8,128)(2,1)S(1)} %copy-done.3, bf16[128]{0:T(256)(128)(2,1)S(1)} %compare_convert_fusion), kind=kOutput, calls=%fused_computation.1 | convolution fusion | flops 537952256 | bytes 6357248 | tf_op jit(solution)/shard_map/dot_general | solution.py:33
  87.5 0.0 copy-start
  87.5 0.0 copy-start.4
  87.5 0.0 reduce-scatter.3.cloned.1.call-update
  88.3 0.0 copy-done.5
  88.4 0.6 dynamic_slice.9
  89.6 0.0 copy-done.1
  89.6 0.0 copy-done.2
  89.7 11.8 %conditional.4 = (f32[256,256]{1,0:T(8,128)S(1)}) conditional(s32[]{:T(128)} %bitcast.6, f32[256,256]{1,0:T(8,128)S(1)} %fusion.12, f32[256,256]{1,0:T(8,128)S(1)} %fusion.12, f32[256,256]{1,0:T(8,128)S(1)} %fusion.12, f32[256,256]{1,0:T(8,128)S(1)} %fusion.12, f32[256,256]{1,0:T(8,128)S(1)} %fusion.12), branch_computations={%region_3.4_spmd, %region_4.5_spmd, %region_5.6_spmd, %region_6.7_... | conditional | flops 131072 | bytes 1310768
  89.7 8.5 %collective-permute-start.4 = (bf16[256,256]{1,0:T(8,128)(2,1)S(1)}, bf16[256,256]{1,0:T(8,128)(2,1)S(1)}, u32[]{:S(2)}, u32[]{:S(2)}) collective-permute-start(bf16[256,256]{1,0:T(8,128)(2,1)S(1)} %convert_element_type.67), channel_id=1, source_target_pairs={{0,512},{32,544},{64,576},{96,608},{128,640},{160,672},{192,704},{... | collective-permute-start | bytes 393224 | tf_op jit(solution)/shard_map/cond/branch_4_fun/ppermute | solution.py:23
  98.2 3.2 %collective-permute-done.4 = bf16[256,256]{1,0:T(8,128)(2,1)S(1)} collective-permute-done((bf16[256,256]{1,0:T(8,128)(2,1)S(1)}, bf16[256,256]{1,0:T(8,128)(2,1)S(1)}, u32[]{:S(2)}, u32[]{:S(2)}) %collective-permute-start.4) | collective-permute-done | bytes 131104 | tf_op jit(solution)/shard_map/cond/branch_4_fun/ppermute | solution.py:23
  101.4 1.9 fusion.16
  103.3 0.0 copy-done
  103.3 0.0 copy-done.4
  103.3 3.6 %fusion.6 = bf16[128,256]{1,0:T(8,128)(2,1)} fusion(bf16[1,8192,256]{2,1,0:T(8,128)(2,1)} %all-gather.3.cloned.1.call-done, bf16[128,8192]{1,0:T(8,128)(2,1)S(1)} %copy-done, f32[8192]{0:T(1024)S(1)} %copy-done.4, f32[128]{0:T(128)S(1)} %add_rsqrt_fusion), kind=kOutput, calls=%fused_computation.10 | convolution fusion | flops 541097984 | bytes 6390272 | tf_op jit(solution)/shard_map/dot_general | solution.py:62
  106.9 39.3 %reduce-scatter.5.cloned.1.call-done = bf16[1024,256]{1,0:T(8,128)(2,1)} async-done(((bf16[8192,256]{1,0:T(8,128)(2,1)}), bf16[1024,256]{1,0:T(8,128)(2,1)}) %reduce-scatter.5.cloned.1.call-update) | async-done | bytes 524304 | tf_op jit(solution)/shard_map/reduce_scatter | solution.py:70
  146.2 58.3 %reduce-scatter.3.cloned.1.call-done = bf16[128,2048]{1,0:T(8,128)(2,1)} async-done(((bf16[128,8192]{1,0:T(8,128)(2,1)}), bf16[128,2048]{1,0:T(8,128)(2,1)}) %reduce-scatter.3.cloned.1.call-update) | async-done | bytes 524304 | tf_op jit(solution)/shard_map/reduce_scatter | solution.py:74
  (4 shorter events, 0.1 us)
Async XLA Ops:
  7.2 75.3 %all-gather.3.cloned.1.call-start = ((), (), s32[]{:S(2)}) async-start(), calls=%async_computation.4 | async-start | bytes 4718592 | tf_op jit(solution)/shard_map/all_gather | solution.py:64
  7.9 138.3 %reduce-scatter.5.cloned.1.call-start = ((), (), s32[]{:S(2)}) async-start(), calls=%async_computation.3 | async-start | bytes 4718592 | tf_op jit(solution)/shard_map/reduce_scatter | solution.py:70
  15.7 66.8 %copy-start.3 = (bf16[128,256]{1,0:T(8,128)(2,1)S(1)}, bf16[128,256]{1,0:T(8,128)(2,1)}, u32[]{:S(2)}) copy-start(bf16[128,256]{1,0:T(8,128)(2,1)} %param.17) | copy-start | bytes 196612
  15.7 72.6 %copy-start.5 = (s32[4]{0:T(128)S(1)}, s32[4]{0:T(128)}, u32[]{:S(2)}) copy-start(s32[4]{0:T(128)} %param.21) | copy-start | bytes 52
  15.7 73.9 %copy-start.1 = (bf16[1,1024,256]{2,1,0:T(8,128)(2,1)S(1)}, bf16[1,1024,256]{2,1,0:T(8,128)(2,1)}, u32[]{:S(2)}) copy-start(bf16[1,1024,256]{2,1,0:T(8,128)(2,1)} %param.16) | copy-start | bytes 1572868
  15.8 73.9 %copy-start.2 = (f32[1,256,256]{2,1,0:T(8,128)S(1)}, f32[1,256,256]{2,1,0:T(8,128)}, u32[]{:S(2)}) copy-start(f32[1,256,256]{2,1,0:T(8,128)} %param.19) | copy-start | bytes 786436
  15.8 188.8 %reduce-scatter.3.cloned.1.call-start = ((), (), s32[]{:S(2)}) async-start(), calls=%async_computation.2 | async-start | bytes 2621440 | tf_op jit(solution)/shard_map/reduce_scatter | solution.py:74
  87.5 15.8 %copy-start = (bf16[128,8192]{1,0:T(8,128)(2,1)S(1)}, bf16[128,8192]{1,0:T(8,128)(2,1)}, u32[]{:S(2)}) copy-start(bf16[128,8192]{1,0:T(8,128)(2,1)} %param.14) | copy-start | bytes 6291460
  87.5 15.8 %copy-start.4 = (f32[8192]{0:T(1024)S(1)}, f32[8192]{0:T(1024)}, u32[]{:S(2)}) copy-start(f32[8192]{0:T(1024)} %param.15) | copy-start | bytes 98308
  89.7 11.7 %collective-permute-start.4 = (bf16[256,256]{1,0:T(8,128)(2,1)S(1)}, bf16[256,256]{1,0:T(8,128)(2,1)S(1)}, u32[]{:S(2)}, u32[]{:S(2)}) collective-permute-start(bf16[256,256]{1,0:T(8,128)(2,1)S(1)} %convert_element_type.67), channel_id=1, source_target_pairs={{0,512},{32,544},{64,576},{96,608},{128,640},{160,672},{192,704},{... | collective-permute-start | bytes 393224 | tf_op jit(solution)/shard_map/cond/branch_4_fun/ppermute | solution.py:23
Sparse Core Ops, SparseCore 0:
  10.7 71.7 all-gather.2
  86.5 59.7 reduce-scatter.4
  150.2 54.2 reduce-scatter.2
where the time goes:
time: 211 us
  waiting for transfers between devices  168 us (80%)
  between operations  15.3 us (7%)
  matrix products  13.7 us (6%)
  starting transfers between devices  8.58 us (4%)
  other arithmetic  4.71 us (2%)
    all_gather x1, waiting for transfers between devices, local(): lax.all_gather(weight, 'fsdp', axis=0, tiled=True)  66.7 us
    reduce_scatter x1, waiting for transfers between devices, local(): lax.psum_scatter(partial_rows.astype(jnp.float32).astype(jnp.bfloat16), '...  58.3 us
    reduce_scatter x1, waiting for transfers between devices, local(): lax.psum_scatter(contract_first(normed, cotan).astype(jnp.bfloat16), 'fsd...  39.3 us
    ppermute x1, starting transfers between devices, swapped(): lax.ppermute(value, axis, [(i, i ^ 1 << bit) for i in range(lax.axis_size...  8.46 us
    dot_general x1, matrix products, contract_last(): lax.dot_general(left, right, (((1,), (1,)), ((), ())), preferred_element_...  5.04 us
    dot_general x1, matrix products, contract_first(): lax.dot_general(left, right, (((0,), (0,)), ((), ())), preferred_element_...  5 us
  transfers between devices with their start and end apart: 4, of which 4 were waited for; matrix products, arithmetic and copies ran while one was open for 9% of the time, Pallas kernels for 0%

commit v1 on v0

v1 whole, which is shorter than its diff:
```python
import functools

import jax
import jax.numpy as jnp
from jax import lax
from jax.experimental import pallas as pl
from jax.experimental.pallas import tpu as pltpu
from jax.sharding import PartitionSpec as P

MESH = pl.DeviceIdType.MESH
PAD = 128004
MU = 0.9
ETA = 0.7
ALPHA = 0.5
NX = 8
NY = 4
BITS = 5
TOK = 128
DF = 1024
HALF = 512
KV = 256
ORDER = (1, 7, 2, 6, 3, 5, 4)


def contract(left, right, dims):
    return lax.dot_general(left, right, (dims, ((), ())), preferred_element_type=jnp.float32)


def kernel(
    plan_ref, frag_ref, ids_ref, x_ref, gain_ref, w_ref, c_ref, anchor_ref, mom_ref,
    value_ref, back_ref, grad_ref, new_anchor_ref, new_mom_ref, merged_ref,
    c_all, xn, xr, part, got, fin, vsend, vr, delta, gossip, inv_ref,
    c_send, c_recv, x_send, x_recv, h_send, h_recv, v_send, v_recv,
    p_send, p_recv, b_send, b_recv, g_send, g_recv,
):
    r = lax.axis_index("replica")
    f = lax.axis_index("fsdp")
    t = lax.axis_index("tensor")
    h = lax.rem(t, 2)
    mate = t + 1 - 2 * h

    def column(offset):
        return lax.rem(f + offset + NX, NX)

    def row(offset):
        return lax.rem(t + offset, NY)

    def partner(bit):
        own = lax.rem(r // (1 << bit), 2)
        return r + (1 << bit) * (1 - 2 * own)

    def push(src, dst, send, recv, **where):
        return pltpu.make_async_remote_copy(
            src_ref=src, dst_ref=dst, send_sem=send, recv_sem=recv, device_id=where, device_id_type=MESH
        )

    home = f // 2
    side = lax.rem(f, 2)
    slots = (t, t + NY)
    homes = [column(-slot) for slot in slots]
    stays = jnp.logical_and(t == 0, home == 0)

    barrier = pltpu.get_barrier_semaphore()

    def greet(**where):
        pl.semaphore_signal(barrier, inc=1, device_id=where, device_id_type=MESH)

    for d in range(1, NX):
        greet(fsdp=column(d))
    for s in range(1, NY):
        greet(tensor=row(s))
    for bit in range(BITS):
        greet(replica=partner(bit))
    for j in range(2):
        origin = 2 * t + j
        gap = lax.rem(origin - f + NX, NX)

        @pl.when(jnp.logical_not(jnp.logical_and(gap == 0, t == 0)))
        def _():
            greet(fsdp=origin, tensor=lax.rem(gap, NY))

    keep = jnp.where(ids_ref[...] != PAD, 1.0, 0.0).astype(jnp.float32)
    keep = jnp.broadcast_to(keep, (TOK, TOK)).T
    for j in range(KV // TOK):
        cols = slice(j * TOK, (j + 1) * TOK)
        c_all[0, :, cols] = (c_ref[:, cols].astype(jnp.float32) * keep).astype(jnp.bfloat16)
    p = frag_ref[0]
    expo = plan_ref[p]
    own_delta = anchor_ref[...] - w_ref[p].astype(jnp.float32)
    delta[...] = own_delta.astype(jnp.bfloat16)

    pl.semaphore_wait(barrier, NX - 1 + NY - 1 + BITS + 2 - jnp.where(stays, 1, 0))

    c_copies = {
        d: push(c_all.at[0], c_all.at[d], c_send.at[d], c_recv.at[d], fsdp=column(d)) for d in ORDER
    }
    for d in ORDER:
        c_copies[d].start()
    g_copies = [
        push(delta, gossip.at[bit], g_send.at[bit], g_recv.at[bit], replica=partner(bit)) for bit in range(BITS)
    ]
    for copy in g_copies:
        copy.start()

    def squares(i, acc):
        start = pl.multiple_of(i * DF, DF)
        block = x_ref[:, pl.ds(start, DF)].astype(jnp.float32)
        for j in range(DF // 128):
            piece = block[:, j * 128 : (j + 1) * 128]
            acc = acc + piece * piece
        return acc

    acc = lax.fori_loop(0, NX, squares, jnp.zeros((TOK, 128), jnp.float32))
    mean = jnp.sum(acc, axis=1, keepdims=True) * (1.0 / (NX * DF))
    inv_ref[...] = jnp.broadcast_to(lax.rsqrt(mean + 1e-05), (TOK, 128))

    def normed(start, width):
        start = pl.multiple_of(start, HALF)
        block = x_ref[:, pl.ds(start, width)].astype(jnp.float32)
        return (block * inv_ref[:, :1] * gain_ref[:, pl.ds(start, width)]).astype(jnp.bfloat16)

    x_copies = {}
    for d in ORDER:
        there = column(d)
        xn[d] = normed(there * DF + h * HALF, HALF)
        x_copies[d] = push(xn.at[d], xr.at[h, d], x_send.at[d], x_recv.at[d], fsdp=there)
        x_copies[d].start()
    for side_h in range(2):
        xr[side_h, 0] = normed(f * DF + side_h * HALF, HALF)

    for d in ORDER:
        c_copies[d].wait_recv()
    weight = w_ref[...].reshape(DF, KV)
    p_copies = []
    for s in (2, 1, 3, 0):
        for j in range(2):
            slot = row(s) + j * NY
            part[s, j] = contract(c_all[slot], weight, ((1,), (1,))).astype(jnp.bfloat16)
        if s:
            copy = push(part.at[s], got.at[s], p_send.at[s], p_recv.at[s], tensor=row(s))
            copy.start()
            p_copies.append(copy)

    def values(d):
        lo = contract(xr[0, d], weight[:HALF], ((1,), (0,)))
        hi = contract(xr[1, d], weight[HALF:], ((1,), (0,)))
        return lo + hi

    h_copies = {}
    for d in ORDER:
        x_copies[d].wait_recv()
        h_copies[d] = push(xr.at[h, d], xr.at[h, d], h_send.at[d], h_recv.at[d], tensor=mate)
        h_copies[d].start()
    v_copies = {}
    for d in ORDER:
        h_copies[d].wait_recv()
        vsend[d] = values(d).astype(jnp.bfloat16)
        v_copies[d] = push(vsend.at[d], vr.at[d], v_send.at[d], v_recv.at[d], fsdp=column(-d))
        v_copies[d].start()

    for copy in g_copies:
        copy.wait_recv()
    own_weight = w_ref[p].astype(jnp.float32)
    anchor = anchor_ref[...]
    mean_delta = 0.5 * (anchor - own_weight + gossip[expo].astype(jnp.float32))
    momentum = MU * mom_ref[...] + mean_delta
    new_anchor = anchor - ETA * (mean_delta + MU * momentum)
    new_mom_ref[...] = momentum
    new_anchor_ref[...] = new_anchor
    merged_ref[...] = (ALPHA * own_weight + (1.0 - ALPHA) * new_anchor).astype(jnp.bfloat16)

    for copy in p_copies:
        copy.wait_recv()
    for j in range(2):
        total = part[0, j].astype(jnp.float32)
        for s in range(1, NY):
            total = total + got[s, j].astype(jnp.float32)
        fin[j] = total.astype(jnp.bfloat16)
    place = back_ref.at[:, pl.ds(pl.multiple_of(side * DF, DF), DF)]
    b_copies = [
        push(fin.at[j], place, b_send.at[j], b_recv.at[side], fsdp=homes[j], tensor=home) for j in range(2)
    ]
    kept = pltpu.make_async_copy(fin.at[0], place, b_recv.at[side])

    @pl.when(stays)
    def _():
        kept.start()

    @pl.when(jnp.logical_not(stays))
    def _():
        b_copies[0].start()

    b_copies[1].start()

    cotan = c_all[...].reshape(NX * TOK, KV)
    for side_h in range(2):
        block = contract(cotan, xr[side_h].reshape(NX * TOK, HALF), ((0,), (0,)))
        grad_ref[side_h * HALF : (side_h + 1) * HALF, :] = block.T.astype(jnp.bfloat16)

    total = values(0)
    for d in ORDER:
        v_copies[d].wait_recv()
        total = total + vr[d].astype(jnp.float32)
    value_ref[...] = total.astype(jnp.bfloat16)

    for j in range(2):
        pltpu.make_async_copy(fin.at[j], back_ref.at[:, j * DF : (j + 1) * DF], b_recv.at[j]).wait()

    @pl.when(jnp.logical_not(stays))
    def _():
        b_copies[0].wait_send()

    b_copies[1].wait_send()
    for d in ORDER:
        c_copies[d].wait_send()
        x_copies[d].wait_send()
        h_copies[d].wait_send()
        v_copies[d].wait_send()
    for copy in p_copies + g_copies:
        copy.wait_send()


def local(
    layer_input, norm_gain, value_weight, value_cotangent, token_ids,
    anchor_weight, outer_momentum, gossip_exponent, fragment_index,
):
    bf16, f32 = jnp.bfloat16, jnp.float32
    smem = pl.BlockSpec(memory_space=pltpu.SMEM)
    vmem = pl.BlockSpec(memory_space=pltpu.VMEM)
    dma = pltpu.SemaphoreType.DMA
    frag = anchor_weight.shape[1:]
    outs = pl.pallas_call(
        kernel,
        out_shape=(
            jax.ShapeDtypeStruct((TOK, KV), bf16),
            jax.ShapeDtypeStruct((TOK, 2 * DF), bf16),
            jax.ShapeDtypeStruct((DF, KV), bf16),
            jax.ShapeDtypeStruct(frag, f32),
            jax.ShapeDtypeStruct(frag, f32),
            jax.ShapeDtypeStruct(frag, bf16),
        ),
        in_specs=[smem, smem] + [vmem] * 7,
        out_specs=[vmem] * 6,
        scratch_shapes=[
            pltpu.VMEM((NX, TOK, KV), bf16),
            pltpu.VMEM((NX, TOK, HALF), bf16),
            pltpu.VMEM((2, NX, TOK, HALF), bf16),
            pltpu.VMEM((NY, 2, TOK, DF), bf16),
            pltpu.VMEM((NY, 2, TOK, DF), bf16),
            pltpu.VMEM((2, TOK, DF), bf16),
            pltpu.VMEM((NX, TOK, KV), bf16),
            pltpu.VMEM((NX, TOK, KV), bf16),
            pltpu.VMEM(frag, bf16),
            pltpu.VMEM((BITS, *frag), bf16),
            pltpu.VMEM((TOK, 128), f32),
            dma((NX,)), dma((NX,)), dma((NX,)), dma((NX,)), dma((NX,)), dma((NX,)), dma((NX,)), dma((NX,)),
            dma((NY,)), dma((NY,)), dma((2,)), dma((2,)), dma((BITS,)), dma((BITS,)),
        ],
        compiler_params=pltpu.CompilerParams(
            collective_id=0, has_side_effects=True, vmem_limit_bytes=48 * 1024 * 1024
        ),
        cost_estimate=pl.CostEstimate(flops=2 * 10**9, bytes_accessed=6 * 10**6, transcendentals=128),
    )(
        gossip_exponent, fragment_index, token_ids.reshape(1, TOK), layer_input, norm_gain.reshape(1, NX * DF),
        value_weight.reshape(4, KV, KV), value_cotangent, anchor_weight[0], outer_momentum[0],
    )
    value, back, grad, new_anchor, new_momentum, merged = outs
    return value, back, grad[None], new_anchor[None], new_momentum[None], merged[None]


def solution(mesh):
    tokens = ("replica", "fsdp")
    whole = P("replica", "fsdp", "tensor")
    return jax.shard_map(
        local,
        mesh=mesh,
        in_specs=(P(tokens, None), P(), whole, P(tokens, "tensor"), P(tokens), whole, whole, P(), P()),
        out_specs=(P(tokens, "tensor"), P(tokens, "tensor"), whole, whole, whole, whole),
        check_vma=False,
    )
```

time: 211 us -> 123 us (0.58)
  the two profiles are of different devices: /device:TPU:1 before, /device:TPU:12 now
where the time goes in v1:
time: 123 us; the launch traced here: 122 us
  Pallas kernels  109 us (89%)
  local copies, waits for them, and re-layouts  11.7 us (10%)
  between operations  1.31 us (1%)
    pallas_call x1, Pallas kernels, local(): pl.pallas_call(kernel, out_shape=(jax.ShapeDtypeStruct((TOK, KV), bf16),...  109 us
    unnamed x22, local copies, waits for them, and re-layouts  11.7 us

profile of v1, /device:TPU:12, one launch (start us, length us, event | category | flops | bytes accessed | tf_op | source)
XLA Modules:
  0.0 122.4 jit_solution(12550957598600902744)
XLA Ops:
  1.3 0.0 copy-start
  1.3 1.6 %copy-done = bf16[128,8192]{1,0:T(8,128)(2,1)S(1)} copy-done((bf16[128,8192]{1,0:T(8,128)(2,1)S(1)}, bf16[128,8192]{1,0:T(8,128)(2,1)}, u32[]{:S(2)}) %copy-start) | copy-done | bytes 2097176
  2.9 0.0 copy-start.1
  2.9 1.0 copy-done.1
  3.9 0.0 copy-start.2
  3.9 0.9 copy-done.2
  4.9 0.0 copy-start.3
  4.9 0.9 copy-done.3
  5.8 0.0 copy-start.4
  5.8 0.8 copy-done.4
  6.7 0.0 copy-start.5
  6.7 0.8 copy-done.5
  7.4 0.0 copy-start.6
  7.4 0.7 copy-done.6
  8.1 0.0 copy-start.7
  8.1 0.7 copy-done.7
  8.7 109.4 %shard_map.136 = (bf16[128,256]{1,0:T(8,128)(2,1)S(1)}, bf16[128,2048]{1,0:T(8,128)(2,1)S(1)}, bf16[1024,256]{1,0:T(8,128)(2,1)S(1)}, f32[256,256]{1,0:T(8,128)S...) custom-call(s32[4]{0:T(128)S(1)} %copy-done.6, s32[1]{0:T(128)S(6)} %copy.21.frag_ref, s32[1,128]{1,0:T(1,128)S(1)} %bitcast.17, ...), custom_call_target="tpu_custom_call" | custom-call | flops 2000000000 | bytes 6000000 | tf_op jit(solution)/shard_map/pallas_call | solution.py:232
  118.1 0.6 copy.22
  118.7 0.8 copy.23
  119.5 0.8 copy.24
  120.3 0.7 copy.25
  121.0 0.7 copy.26
  121.7 0.7 copy.27
Async XLA Ops:
  1.3 1.6 %copy-start = (bf16[128,8192]{1,0:T(8,128)(2,1)S(1)}, bf16[128,8192]{1,0:T(8,128)(2,1)}, u32[]{:S(2)}) copy-start(bf16[128,8192]{1,0:T(8,128)(2,1)} %x_ref.1) | copy-start | bytes 6291460
  2.9 1.0 copy-start.1
  3.9 0.9 copy-start.2
  4.9 0.9 copy-start.3
  5.8 0.8 copy-start.4
  6.7 0.8 copy-start.5
  7.4 0.7 copy-start.6
  8.1 0.7 copy-start.7

commit v2 on v1

v2 whole, which is shorter than its diff:
```python
import functools

import jax
import jax.numpy as jnp
from jax import lax
from jax.experimental import pallas as pl
from jax.experimental.pallas import tpu as pltpu
from jax.sharding import PartitionSpec as P

MESH = pl.DeviceIdType.MESH
PAD = 128004
MU = 0.9
ETA = 0.7
ALPHA = 0.5
NX = 8
NY = 4
BITS = 5
TOK = 128
DF = 1024
HALF = 512
KV = 256
ORDER = (1, 7, 2, 6, 3, 5, 4)


def contract(left, right, dims):
    return lax.dot_general(left, right, (dims, ((), ())), preferred_element_type=jnp.float32)


def kernel(
    plan_ref, frag_ref, ids_hbm, x_hbm, gain_hbm, w_hbm, c_hbm, anchor_hbm, mom_hbm,
    value_ref, back_ref, grad_ref, new_anchor_ref, new_mom_ref, merged_ref,
    ids_ref, x_ref, gain_ref, w_ref, c_ref, anchor_ref, mom_ref,
    c_all, c_four, w_all, xn, xr, fin, vsend, vr, delta, gossip, inv_ref,
    load, c_send, c_recv, cy_send, cy_recv, four_send, four_recv, w_send, w_recv,
    x_send, near_send, near_recv, far_send, far_recv, v_send, v_recv, b_send, b_recv, g_send, g_recv,
):
    r = lax.axis_index("replica")
    f = lax.axis_index("fsdp")
    t = lax.axis_index("tensor")
    h = t // 2
    inward = t + 1 - 2 * h
    outward = t - 1 + 2 * h
    middle = jnp.logical_or(t == 1, t == 2)
    end = jnp.logical_not(middle)

    def column(offset):
        return lax.rem(f + offset + NX, NX)

    def partner(bit):
        own = lax.rem(r // (1 << bit), 2)
        return r + (1 << bit) * (1 - 2 * own)

    def push(src, dst, send, recv, **where):
        return pltpu.make_async_remote_copy(
            src_ref=src, dst_ref=dst, send_sem=send, recv_sem=recv, device_id=where, device_id_type=MESH
        )

    w_own = w_all.at[t]
    pairs = (
        (c_hbm, c_ref), (ids_hbm, ids_ref), (w_hbm, w_own), (x_hbm, x_ref), (gain_hbm, gain_ref),
        (anchor_hbm, anchor_ref), (mom_hbm, mom_ref), (w_hbm, w_ref),
    )
    loads = [pltpu.make_async_copy(src, dst, load.at[i]) for i, (src, dst) in enumerate(pairs)]
    for copy in loads:
        copy.start()

    home = f // 2
    side = lax.rem(f, 2)
    stays = jnp.logical_and(t == 1, home == 1)

    barrier = pltpu.get_barrier_semaphore()

    def greet(**where):
        pl.semaphore_signal(barrier, inc=1, device_id=where, device_id_type=MESH)

    greet(tensor=inward)
    for d in range(1, NX):
        greet(fsdp=column(d))
    for bit in range(BITS):
        greet(replica=partner(bit))

    @pl.when(middle)
    def _():
        greet(tensor=outward)
        greet(tensor=3 * (1 - h))

    for j in range(2):
        origin = 2 * t + j
        gap = lax.rem(origin - f + NX, NX)

        @pl.when(jnp.logical_not(jnp.logical_and(gap == 0, t == 1)))
        def _():
            greet(fsdp=origin, tensor=1 + lax.rem(gap, 2))

    loads[0].wait()
    loads[1].wait()
    keep = jnp.where(ids_ref[...] != PAD, 1.0, 0.0).astype(jnp.float32)
    keep = jnp.broadcast_to(keep, (TOK, TOK)).T
    for j in range(KV // TOK):
        cols = slice(j * TOK, (j + 1) * TOK)
        c_all[0, :, cols] = (c_ref[:, cols].astype(jnp.float32) * keep).astype(jnp.bfloat16)
    loads[2].wait()

    pl.semaphore_wait(barrier, NX - 1 + BITS + 2 + jnp.where(middle, 4, 0) - jnp.where(stays, 1, 0))

    c_copies = {d: push(c_all.at[0], c_all.at[d], c_send.at[d], c_recv.at[d], fsdp=column(d)) for d in ORDER}
    cy_in = push(c_all.at[0], c_four.at[NY, t], cy_send.at[0], cy_recv.at[t], tensor=inward)
    cy_over = push(c_all.at[0], c_four.at[NY, t], cy_send.at[1], cy_recv.at[t], tensor=2 - h)
    four = [
        push(c_four.at[NY], c_four.at[i], four_send.at[i], four_recv.at[i], fsdp=column(d))
        for i, d in enumerate((0, 2, 4, 6))
    ]
    four_odd = [
        push(c_four.at[NY], c_four.at[i], four_send.at[i], four_recv.at[i], fsdp=column(d))
        for i, d in enumerate((1, 3, 5, 7))
    ]
    w_in = push(w_own, w_own, w_send.at[0], w_recv.at[t], tensor=inward)
    w_pass = push(w_all.at[outward], w_all.at[outward], w_send.at[1], w_recv.at[outward], tensor=inward)
    near_in = {d: push(xr.at[h, d], xr.at[h, d], near_send.at[d], near_recv.at[d], tensor=inward) for d in ORDER}
    near_across = {d: push(xr.at[h, d], xr.at[h, d], near_send.at[d], far_recv.at[d], tensor=inward) for d in ORDER}
    far_out = {
        d: push(xr.at[1 - h, d], xr.at[1 - h, d], far_send.at[d], far_recv.at[d], tensor=outward) for d in ORDER
    }
    x_copies = {d: push(xn.at[d], xr.at[h, d], x_send.at[d], near_recv.at[d], fsdp=column(d)) for d in ORDER}
    v_copies = {d: push(vsend.at[d], vr.at[d], v_send.at[d], v_recv.at[d], fsdp=column(-d)) for d in ORDER}
    g_copies = [
        push(delta, gossip.at[bit], g_send.at[bit], g_recv.at[bit], replica=partner(bit)) for bit in range(BITS)
    ]
    place = back_ref.at[:, pl.ds(pl.multiple_of(side * DF, DF), DF)]

    def norm_scale():
        def squares(i, acc):
            start = pl.multiple_of(i * DF, DF)
            block = x_ref[:, pl.ds(start, DF)].astype(jnp.float32)
            for j in range(DF // 128):
                piece = block[:, j * 128 : (j + 1) * 128]
                acc = acc + piece * piece
            return acc

        loads[3].wait()
        loads[4].wait()
        acc = lax.fori_loop(0, NX, squares, jnp.zeros((TOK, 128), jnp.float32))
        mean = jnp.sum(acc, axis=1, keepdims=True) * (1.0 / (NX * DF))
        inv_ref[...] = jnp.broadcast_to(lax.rsqrt(mean + 1e-05), (TOK, 128))

    def normed(start):
        start = pl.multiple_of(start, HALF)
        block = x_ref[:, pl.ds(start, HALF)].astype(jnp.float32)
        return (block * inv_ref[:, :1] * gain_ref[:, pl.ds(start, HALF)]).astype(jnp.bfloat16)

    def own_tokens():
        for j in range(2):
            xr[j, 0] = normed(f * DF + j * HALF)

    p = frag_ref[0]

    def send_delta():
        loads[5].wait()
        loads[6].wait()
        loads[7].wait()
        delta[...] = (anchor_ref[...] - w_ref[p].astype(jnp.float32)).astype(jnp.bfloat16)
        for copy in g_copies:
            copy.start()

    def values(d):
        weight = w_ref[...].reshape(DF, KV)
        lo = contract(xr[0, d], weight[:HALF], ((1,), (0,)))
        hi = contract(xr[1, d], weight[HALF:], ((1,), (0,)))
        return lo + hi

    def send_values(d):
        vsend[d] = values(d).astype(jnp.bfloat16)
        v_copies[d].start()

    @pl.when(end)
    def _():
        w_in.start()
        cy_in.start()
        cy_over.start()
        for d in ORDER:
            c_copies[d].start()
        norm_scale()
        for d in ORDER:
            xn[d] = normed(column(d) * DF + h * HALF)
            x_copies[d].start()
        own_tokens()
        send_delta()
        for d in ORDER:
            x_copies[d].wait_recv()
            near_in[d].start()
        for d in ORDER:
            far_out[d].wait_recv()
            send_values(d)
        for d in ORDER:
            c_copies[d].wait_recv()

    def middle_row(row):
        parity = row - 1
        slots = [d for d in (0, *ORDER) if d % 2 == parity]
        others = [d for d in ORDER if d % 2 != parity]
        fours = dict(zip((parity, parity + 2, parity + 4, parity + 6), (four_odd if parity else four)))
        back = {
            d: push(fin.at[d // 2], place, b_send.at[d // 2], b_recv.at[side], fsdp=column(-d), tensor=home)
            for d in slots
        }
        kept = pltpu.make_async_copy(fin.at[0], place, b_recv.at[side])

        def finish(d):
            if d:
                fours[d].wait_recv()
                c_all[d] = c_four[d // 2, row]
            held = d // 2 if d else NY
            total = jnp.zeros((TOK, DF), jnp.float32)
            for block in range(NY):
                total = total + contract(c_four[held, block], w_all[block].reshape(DF, KV), ((1,), (1,)))
            fin[d // 2] = total.astype(jnp.bfloat16)
            if d:
                back[d].start()
            else:

                @pl.when(stays)
                def _():
                    kept.start()

                @pl.when(jnp.logical_not(stays))
                def _():
                    back[0].start()

        cy_in.start()
        w_in.start()
        c_four[NY, row] = c_all[0]
        for block in range(NY):
            if block != row:
                push(c_all.at[0], c_four.at[NY, block], cy_send.at[0], cy_recv.at[block], tensor=inward).wait_recv()
        for d in slots:
            if d:
                fours[d].start()
        for d in others:
            c_copies[d].start()
        norm_scale()
        own_tokens()
        send_delta()
        push(w_own, w_all.at[outward], w_send.at[0], w_recv.at[outward], tensor=inward).wait_recv()
        w_pass.start()
        lag = 2
        for step in range(len(ORDER) + lag):
            if step < len(ORDER):
                near_in[ORDER[step]].wait_recv()
                near_across[ORDER[step]].start()
            if step == 3:
                push(w_own, w_all.at[inward], w_send.at[0], w_recv.at[inward], tensor=inward).wait_recv()
                past = 3 * (1 - h)
                push(w_own, w_all.at[past], w_send.at[0], w_recv.at[past], tensor=inward).wait_recv()
            if 3 <= step < 7:
                finish(slots[step - 3])
            if step >= lag:
                d = ORDER[step - lag]
                far_out[d].wait_recv()
                far_out[d].start()
                send_values(d)
        for d in others:
            c_copies[d].wait_recv()
        for d in others:
            c_copies[d].wait_send()
        for d in slots:
            if d:
                fours[d].wait_send()
                back[d].wait_send()
        if 0 in slots:

            @pl.when(jnp.logical_not(stays))
            def _():
                back[0].wait_send()

    for row in (1, 2):
        pl.when(t == row)(functools.partial(middle_row, row))

    for copy in g_copies:
        copy.wait_recv()
    expo = plan_ref[p]
    own_weight = w_ref[p].astype(jnp.float32)
    anchor = anchor_ref[...]
    mean_delta = 0.5 * (anchor - own_weight + gossip[expo].astype(jnp.float32))
    momentum = MU * mom_ref[...] + mean_delta
    new_anchor = anchor - ETA * (mean_delta + MU * momentum)
    new_mom_ref[...] = momentum
    new_anchor_ref[...] = new_anchor
    merged_ref[...] = (ALPHA * own_weight + (1.0 - ALPHA) * new_anchor).astype(jnp.bfloat16)

    cotan = c_all[...].reshape(NX * TOK, KV)
    for j in range(2):
        block = contract(cotan, xr[j].reshape(NX * TOK, HALF), ((0,), (0,)))
        grad_ref[j * HALF : (j + 1) * HALF, :] = block.T.astype(jnp.bfloat16)

    total = values(0)
    for d in ORDER:
        v_copies[d].wait_recv()
        total = total + vr[d].astype(jnp.float32)
    value_ref[...] = total.astype(jnp.bfloat16)

    for j in range(2):
        pltpu.make_async_copy(fin.at[j], back_ref.at[:, j * DF : (j + 1) * DF], b_recv.at[j]).wait()

    w_in.wait_send()
    cy_in.wait_send()
    for d in ORDER:
        near_in[d].wait_send()
        v_copies[d].wait_send()
    for copy in g_copies:
        copy.wait_send()

    @pl.when(end)
    def _():
        cy_over.wait_send()
        for d in ORDER:
            c_copies[d].wait_send()
            x_copies[d].wait_send()

    @pl.when(middle)
    def _():
        w_pass.wait_send()
        for d in ORDER:
            far_out[d].wait_send()


def write_out(*refs):
    n = len(refs) // 2
    copies = [pltpu.make_async_copy(refs[i], refs[n + i], refs[-1].at[i]) for i in range(n)]
    for copy in copies:
        copy.start()
    for copy in copies:
        copy.wait()


def local(
    layer_input, norm_gain, value_weight, value_cotangent, token_ids,
    anchor_weight, outer_momentum, gossip_exponent, fragment_index,
):
    bf16, f32 = jnp.bfloat16, jnp.float32
    smem = pl.BlockSpec(memory_space=pltpu.SMEM)
    vmem = pl.BlockSpec(memory_space=pltpu.VMEM)
    anywhere = pl.BlockSpec(memory_space=pl.ANY)
    dma = pltpu.SemaphoreType.DMA
    frag = anchor_weight.shape[1:]
    shapes = (
        jax.ShapeDtypeStruct((TOK, KV), bf16),
        jax.ShapeDtypeStruct((TOK, 2 * DF), bf16),
        jax.ShapeDtypeStruct((DF, KV), bf16),
        jax.ShapeDtypeStruct(frag, f32),
        jax.ShapeDtypeStruct(frag, f32),
        jax.ShapeDtypeStruct(frag, bf16),
    )
    outs = pl.pallas_call(
        kernel,
        out_shape=shapes,
        in_specs=[smem, smem] + [anywhere] * 7,
        out_specs=[vmem] * 6,
        scratch_shapes=[
            pltpu.VMEM((1, TOK), jnp.int32),
            pltpu.VMEM((TOK, NX * DF), bf16),
            pltpu.VMEM((1, NX * DF), f32),
            pltpu.VMEM((4, KV, KV), bf16),
            pltpu.VMEM((TOK, KV), bf16),
            pltpu.VMEM(frag, f32),
            pltpu.VMEM(frag, f32),
            pltpu.VMEM((NX, TOK, KV), bf16),
            pltpu.VMEM((NY + 1, NY, TOK, KV), bf16),
            pltpu.VMEM((NY, 4, KV, KV), bf16),
            pltpu.VMEM((NX, TOK, HALF), bf16),
            pltpu.VMEM((2, NX, TOK, HALF), bf16),
            pltpu.VMEM((4, TOK, DF), bf16),
            pltpu.VMEM((NX, TOK, KV), bf16),
            pltpu.VMEM((NX, TOK, KV), bf16),
            pltpu.VMEM(frag, bf16),
            pltpu.VMEM((BITS, *frag), bf16),
            pltpu.VMEM((TOK, 128), f32),
            dma((8,)), dma((NX,)), dma((NX,)), dma((2,)), dma((NY,)), dma((4,)), dma((4,)), dma((2,)), dma((NY,)),
            dma((NX,)), dma((NX,)), dma((NX,)), dma((NX,)), dma((NX,)),
            dma((NX,)), dma((NX,)), dma((4,)), dma((2,)), dma((BITS,)), dma((BITS,)),
        ],
        compiler_params=pltpu.CompilerParams(
            collective_id=0, has_side_effects=True, vmem_limit_bytes=56 * 1024 * 1024
        ),
        cost_estimate=pl.CostEstimate(flops=2 * 10**9, bytes_accessed=6 * 10**6, transcendentals=128),
    )(
        gossip_exponent, fragment_index, token_ids.reshape(1, TOK), layer_input, norm_gain.reshape(1, NX * DF),
        value_weight.reshape(4, KV, KV), value_cotangent, anchor_weight[0], outer_momentum[0],
    )
    outs = pl.pallas_call(
        write_out,
        out_shape=shapes,
        in_specs=[vmem] * 6,
        out_specs=[anywhere] * 6,
        scratch_shapes=[dma((6,))],
    )(*outs)
    value, back, grad, new_anchor, new_momentum, merged = outs
    return value, back, grad[None], new_anchor[None], new_momentum[None], merged[None]


def solution(mesh):
    tokens = ("replica", "fsdp")
    whole = P("replica", "fsdp", "tensor")
    return jax.shard_map(
        local,
        mesh=mesh,
        in_specs=(P(tokens, None), P(), whole, P(tokens, "tensor"), P(tokens), whole, whole, P(), P()),
        out_specs=(P(tokens, "tensor"), P(tokens, "tensor"), whole, whole, whole, whole),
        check_vma=False,
    )
```

time: 123 us -> 104 us (0.85)
  the two profiles are of different devices: /device:TPU:12 before, /device:TPU:1 now
where the time goes in v2:
time: 104 us; the launch traced here: 102 us
  Pallas kernels  101 us (97%)
  between operations  1.29 us (1%)
    pallas_call x1, Pallas kernels, local(): pl.pallas_call(kernel, out_shape=shapes, in_specs=[smem, smem] + [anywher...  98.5 us
    pallas_call x1, Pallas kernels, local(): pl.pallas_call(write_out, out_shape=shapes, in_specs=[vmem] * 6, out_spec...  2.65 us

profile of v2, /device:TPU:1, one launch (start us, length us, event | category | flops | bytes accessed | tf_op | source)
XLA Modules:
  0.0 102.5 jit_solution(8408269041480002383)
XLA Ops:
  1.3 98.5 %shard_map.136 = (bf16[128,256]{1,0:T(8,128)(2,1)}, bf16[128,2048]{1,0:T(8,128)(2,1)}, bf16[1024,256]{1,0:T(8,128)(2,1)}, f32[256,256]{1,0:T(8,128)}, f32[256,256]{1,0:T(8,128)}, /*index=5*/bf16[256,256]{1,0:T(8,128)(2,1)}) custom-call(s32[4]{0:T(128)} %plan_ref.1, s32[1]{0:T(128)S(6)} %copy.15.frag_ref, s32[1,128]{1,0:T(1,128)} %bitcast.17, ...), custom_call_target="tpu_custom_call" | custom-call | flops 2000000000 | bytes 6000000 | tf_op jit(solution)/shard_map/pallas_call | solution.py:353
  99.8 2.6 %shard_map.137 = (bf16[128,256]{1,0:T(8,128)(2,1)}, bf16[128,2048]{1,0:T(8,128)(2,1)}, bf16[1024,256]{1,0:T(8,128)(2,1)}, f32[256,256]{1,0:T(8,128)}, f32[256,256]{1,0:T(8,128)}, /*index=5*/bf16[256,256]{1,0:T(8,128)(2,1)}) custom-call(bf16[128,256]{1,0:T(8,128)(2,1)} %get-tuple-element.18.refs_0_, bf16[128,2048]{1,0:T(8,128)(2,1)} %get-tuple-element.19.refs_1_, ...), custom_call_target="tpu_custom_call" | custom-call | tf_op jit(solution)/shard_map/pallas_call | solution.py:389

commit v3 on v2

v3 whole, which is shorter than its diff:
```python
import functools

import jax
import jax.numpy as jnp
from jax import lax
from jax.experimental import pallas as pl
from jax.experimental.pallas import tpu as pltpu
from jax.sharding import PartitionSpec as P

MESH = pl.DeviceIdType.MESH
PAD = 128004
MU = 0.9
ETA = 0.7
ALPHA = 0.5
NX = 8
NY = 4
BITS = 5
TOK = 128
DF = 1024
HALF = 512
KV = 256
LAG = 2


def near_first(step):
    return 1 + step // 2 + lax.rem(step, 2) * (6 - 2 * (step // 2))


def each(count, body):
    def step(i, nothing):
        body(i)
        return nothing

    lax.fori_loop(0, count, step, 0)


def contract(left, right, dims):
    return lax.dot_general(left, right, (dims, ((), ())), preferred_element_type=jnp.float32)


def kernel(
    bit,
    frag_ref, ids_hbm, x_hbm, gain_hbm, w_hbm, c_hbm, anchor_hbm, mom_hbm,
    value_ref, back_ref, grad_ref, new_anchor_ref, new_mom_ref, merged_ref,
    ids_ref, x_ref, gain_ref, w_ref, c_ref, anchor_ref, mom_ref,
    c_all, c_four, w_all, xn, xr, acc_ref, fin, vsend, vr, delta, gossip, inv_ref,
    load, c_send, c_recv, cy_send, cy_recv, four_send, four_recv, w_send, w_recv,
    x_send, near_send, near_recv, far_send, far_recv, v_send, v_recv, b_send, b_recv, g_send, g_recv,
):
    r = lax.axis_index("replica")
    f = lax.axis_index("fsdp")
    t = lax.axis_index("tensor")
    h = t // 2
    inward = t + 1 - 2 * h
    outward = t - 1 + 2 * h
    middle = jnp.logical_or(t == 1, t == 2)
    end = jnp.logical_not(middle)

    def column(offset):
        return lax.rem(f + offset + NX, NX)

    partner = r + (1 << bit) * (1 - 2 * lax.rem(r // (1 << bit), 2))

    def push(src, dst, send, recv, **where):
        return pltpu.make_async_remote_copy(
            src_ref=src, dst_ref=dst, send_sem=send, recv_sem=recv, device_id=where, device_id_type=MESH
        )

    w_own = w_all.at[t]
    pairs = (
        (c_hbm, c_ref), (ids_hbm, ids_ref), (w_hbm, w_own), (x_hbm, x_ref), (gain_hbm, gain_ref),
        (anchor_hbm, anchor_ref), (mom_hbm, mom_ref), (w_hbm, w_ref),
    )
    loads = [pltpu.make_async_copy(src, dst, load.at[i]) for i, (src, dst) in enumerate(pairs)]
    for copy in loads:
        copy.start()

    home = f // 2
    side = lax.rem(f, 2)
    stays = jnp.logical_and(t == 1, home == 1)

    barrier = pltpu.get_barrier_semaphore()

    def greet(**where):
        pl.semaphore_signal(barrier, inc=1, device_id=where, device_id_type=MESH)

    greet(tensor=inward)
    for d in range(1, NX):
        greet(fsdp=column(d))
    greet(replica=partner)

    @pl.when(middle)
    def _():
        greet(tensor=outward)
        greet(tensor=3 * (1 - h))

    for j in range(2):
        origin = 2 * t + j
        gap = lax.rem(origin - f + NX, NX)

        @pl.when(jnp.logical_not(jnp.logical_and(gap == 0, t == 1)))
        def _():
            greet(fsdp=origin, tensor=1 + lax.rem(gap, 2))

    loads[0].wait()
    loads[1].wait()
    keep = jnp.where(ids_ref[...] != PAD, 1.0, 0.0).astype(jnp.float32)
    keep = jnp.broadcast_to(keep, (TOK, TOK)).T
    for j in range(KV // TOK):
        cols = slice(j * TOK, (j + 1) * TOK)
        c_all[0, :, cols] = (c_ref[:, cols].astype(jnp.float32) * keep).astype(jnp.bfloat16)
    loads[2].wait()

    pl.semaphore_wait(barrier, NX + 2 + jnp.where(middle, 4, 0) - jnp.where(stays, 1, 0))

    def c_copy(d):
        return push(c_all.at[0], c_all.at[d], c_send.at[d], c_recv.at[d], fsdp=column(d))

    def four_copy(d):
        return push(c_four.at[NY], c_four.at[d // 2], four_send.at[d // 2], four_recv.at[d // 2], fsdp=column(d))

    def near_in(d):
        return push(xr.at[h, d], xr.at[h, d], near_send.at[d], near_recv.at[d], tensor=inward)

    def near_across(d):
        return push(xr.at[h, d], xr.at[h, d], near_send.at[d], far_recv.at[d], tensor=inward)

    def far_out(d):
        return push(xr.at[1 - h, d], xr.at[1 - h, d], far_send.at[d], far_recv.at[d], tensor=outward)

    def x_copy(d):
        return push(xn.at[d], xr.at[h, d], x_send.at[d], near_recv.at[d], fsdp=column(d))

    def v_copy(d):
        return push(vsend.at[d], vr.at[d], v_send.at[d], v_recv.at[d], fsdp=column(-d))

    def back_copy(d):
        return push(fin.at[d // 2], place, b_send.at[d // 2], b_recv.at[side], fsdp=column(-d), tensor=home)

    cy_in = push(c_all.at[0], c_four.at[NY, t], cy_send.at[0], cy_recv.at[t], tensor=inward)
    cy_over = push(c_all.at[0], c_four.at[NY, t], cy_send.at[1], cy_recv.at[t], tensor=2 - h)
    w_in = push(w_own, w_own, w_send.at[0], w_recv.at[t], tensor=inward)
    w_pass = push(w_all.at[outward], w_all.at[outward], w_send.at[1], w_recv.at[outward], tensor=inward)
    g_copy = push(delta, gossip, g_send, g_recv, replica=partner)
    place = back_ref.at[:, pl.ds(pl.multiple_of(side * DF, DF), DF)]

    def norm_scale():
        def squares(i, acc):
            start = pl.multiple_of(i * DF, DF)
            block = x_ref[:, pl.ds(start, DF)].astype(jnp.float32)
            for j in range(DF // 128):
                piece = block[:, j * 128 : (j + 1) * 128]
                acc = acc + piece * piece
            return acc

        loads[3].wait()
        loads[4].wait()
        acc = lax.fori_loop(0, NX, squares, jnp.zeros((TOK, 128), jnp.float32))
        mean = jnp.sum(acc, axis=1, keepdims=True) * (1.0 / (NX * DF))
        inv_ref[...] = jnp.broadcast_to(lax.rsqrt(mean + 1e-05), (TOK, 128))

    def normed(start):
        start = pl.multiple_of(start, HALF)
        block = x_ref[:, pl.ds(start, HALF)].astype(jnp.float32)
        return (block * inv_ref[:, :1] * gain_ref[:, pl.ds(start, HALF)]).astype(jnp.bfloat16)

    def own_tokens():
        for j in range(2):
            xr[j, 0] = normed(f * DF + j * HALF)

    p = frag_ref[0]

    def send_delta():
        loads[5].wait()
        loads[6].wait()
        loads[7].wait()
        delta[...] = (anchor_ref[...] - w_ref[p].astype(jnp.float32)).astype(jnp.bfloat16)
        g_copy.start()

    def values(d):
        weight = w_ref[...].reshape(DF, KV)
        lo = contract(xr[0, d], weight[:HALF], ((1,), (0,)))
        hi = contract(xr[1, d], weight[HALF:], ((1,), (0,)))
        return lo + hi

    def send_values(d):
        vsend[d] = values(d).astype(jnp.bfloat16)
        v_copy(d).start()

    @pl.when(end)
    def _():
        w_in.start()
        cy_in.start()
        cy_over.start()
        norm_scale()

        def spread(step):
            d = near_first(step)
            xn[d] = normed(column(d) * DF + h * HALF)
            x_copy(d).start()

        each(NX - 1, spread)
        each(NX - 1, lambda step: c_copy(near_first(step)).start())
        own_tokens()
        send_delta()

        def onward(step):
            d = near_first(step)
            x_copy(d).wait_recv()
            near_in(d).start()

        each(NX - 1, onward)

        def arrived(step):
            d = near_first(step)
            far_out(d).wait_recv()
            send_values(d)

        each(NX - 1, arrived)
        each(NX - 1, lambda step: c_copy(near_first(step)).wait_recv())

    odd = jnp.where(t == 2, 1, 0)

    def finish(n):
        even_slot = jnp.where(n == 3, 4, jnp.where(n == 2, 6, 2 * n))
        odd_slot = jnp.where(n == 3, 5, jnp.where(n == 2, 3, 1 + 6 * n))
        d = jnp.where(odd == 1, odd_slot, even_slot)

        @pl.when(d != 0)
        def _():
            four_copy(d).wait_recv()
            c_all[d] = c_four[d // 2, t]

        held = jnp.where(d == 0, NY, d // 2)

        def add(block):
            acc_ref[...] += contract(c_four[held, block], w_all[block].reshape(DF, KV), ((1,), (1,)))

        acc_ref[...] = jnp.zeros((TOK, DF), jnp.float32)
        each(NY, add)
        fin[d // 2] = acc_ref[...].astype(jnp.bfloat16)
        here = jnp.logical_and(d == 0, stays)

        @pl.when(here)
        def _():
            pltpu.make_async_copy(fin.at[0], place, b_recv.at[side]).start()

        @pl.when(jnp.logical_not(here))
        def _():
            back_copy(d).start()

    @pl.when(middle)
    def _():
        cy_in.start()
        w_in.start()
        c_four[NY, t] = c_all[0]
        for s in range(1, NY):
            row = lax.rem(t + s, NY)
            push(c_all.at[0], c_four.at[NY, row], cy_send.at[0], cy_recv.at[row], tensor=inward).wait_recv()
        for i in (0, 3, 1, 2):
            mine = 2 * i + odd

            @pl.when(mine != 0)
            def _():
                four_copy(mine).start()

        for i in (0, 3, 1, 2):
            other = 2 * i + 1 - odd

            @pl.when(other != 0)
            def _():
                c_copy(other).start()

        norm_scale()
        own_tokens()
        send_delta()
        push(w_own, w_all.at[outward], w_send.at[0], w_recv.at[outward], tensor=inward).wait_recv()
        w_pass.start()

        def step_of(step):
            @pl.when(step < NX - 1)
            def _():
                d = near_first(step)
                near_in(d).wait_recv()
                near_across(d).start()

            @pl.when(step == 3)
            def _():
                push(w_own, w_all.at[inward], w_send.at[0], w_recv.at[inward], tensor=inward).wait_recv()
                past = 3 * (1 - h)
                push(w_own, w_all.at[past], w_send.at[0], w_recv.at[past], tensor=inward).wait_recv()

            @pl.when(jnp.logical_and(step >= 3, step < NX - 1))
            def _():
                finish(step - 3)

            @pl.when(step >= LAG)
            def _():
                d = near_first(step - LAG)
                far_out(d).wait_recv()
                far_out(d).start()
                send_values(d)

        each(NX - 1 + LAG, step_of)
        for i in range(4):
            mine = 2 * i + odd
            other = 2 * i + 1 - odd

            @pl.when(other != 0)
            def _():
                c_copy(other).wait_recv()
                c_copy(other).wait_send()

            @pl.when(mine != 0)
            def _():
                four_copy(mine).wait_send()

            @pl.when(jnp.logical_not(jnp.logical_and(mine == 0, stays)))
            def _():
                back_copy(mine).wait_send()

    g_copy.wait_recv()
    own_weight = w_ref[p].astype(jnp.float32)
    anchor = anchor_ref[...]
    mean_delta = 0.5 * (anchor - own_weight + gossip[...].astype(jnp.float32))
    momentum = MU * mom_ref[...] + mean_delta
    new_anchor = anchor - ETA * (mean_delta + MU * momentum)
    new_mom_ref[...] = momentum
    new_anchor_ref[...] = new_anchor
    merged_ref[...] = (ALPHA * own_weight + (1.0 - ALPHA) * new_anchor).astype(jnp.bfloat16)

    cotan = c_all[...].reshape(NX * TOK, KV)

    def whole(j):
        block = contract(cotan, xr[j].reshape(NX * TOK, HALF), ((0,), (0,)))
        grad_ref[pl.ds(pl.multiple_of(j * HALF, HALF), HALF), :] = block.T.astype(jnp.bfloat16)

    each(2, whole)
    total = values(0)
    for d in range(1, NX):
        v_copy(d).wait_recv()
        total = total + vr[d].astype(jnp.float32)
    value_ref[...] = total.astype(jnp.bfloat16)

    for j in range(2):
        pltpu.make_async_copy(fin.at[j], back_ref.at[:, j * DF : (j + 1) * DF], b_recv.at[j]).wait()

    w_in.wait_send()
    cy_in.wait_send()
    for d in range(1, NX):
        near_in(d).wait_send()
        v_copy(d).wait_send()
    g_copy.wait_send()

    @pl.when(end)
    def _():
        cy_over.wait_send()
        for d in range(1, NX):
            c_copy(d).wait_send()
            x_copy(d).wait_send()

    @pl.when(middle)
    def _():
        w_pass.wait_send()
        for d in range(1, NX):
            far_out(d).wait_send()


def write_out(*refs):
    n = len(refs) // 2
    copies = [pltpu.make_async_copy(refs[i], refs[n + i], refs[-1].at[i]) for i in range(n)]
    for copy in copies:
        copy.start()
    for copy in copies:
        copy.wait()


def local(
    layer_input, norm_gain, value_weight, value_cotangent, token_ids,
    anchor_weight, outer_momentum, gossip_exponent, fragment_index,
):
    bf16, f32 = jnp.bfloat16, jnp.float32
    smem = pl.BlockSpec(memory_space=pltpu.SMEM)
    vmem = pl.BlockSpec(memory_space=pltpu.VMEM)
    anywhere = pl.BlockSpec(memory_space=pl.ANY)
    dma = pltpu.SemaphoreType.DMA
    frag = anchor_weight.shape[1:]
    shapes = (
        jax.ShapeDtypeStruct((TOK, KV), bf16),
        jax.ShapeDtypeStruct((TOK, 2 * DF), bf16),
        jax.ShapeDtypeStruct((DF, KV), bf16),
        jax.ShapeDtypeStruct(frag, f32),
        jax.ShapeDtypeStruct(frag, f32),
        jax.ShapeDtypeStruct(frag, bf16),
    )
    build = lambda bit: pl.pallas_call(
        functools.partial(kernel, bit),
        out_shape=shapes,
        in_specs=[smem] + [anywhere] * 7,
        out_specs=[vmem] * 6,
        scratch_shapes=[
            pltpu.VMEM((1, TOK), jnp.int32),
            pltpu.VMEM((TOK, NX * DF), bf16),
            pltpu.VMEM((1, NX * DF), f32),
            pltpu.VMEM((4, KV, KV), bf16),
            pltpu.VMEM((TOK, KV), bf16),
            pltpu.VMEM(frag, f32),
            pltpu.VMEM(frag, f32),
            pltpu.VMEM((NX, TOK, KV), bf16),
            pltpu.VMEM((NY + 1, NY, TOK, KV), bf16),
            pltpu.VMEM((NY, 4, KV, KV), bf16),
            pltpu.VMEM((NX, TOK, HALF), bf16),
            pltpu.VMEM((2, NX, TOK, HALF), bf16),
            pltpu.VMEM((TOK, DF), f32),
            pltpu.VMEM((4, TOK, DF), bf16),
            pltpu.VMEM((NX, TOK, KV), bf16),
            pltpu.VMEM((NX, TOK, KV), bf16),
            pltpu.VMEM(frag, bf16),
            pltpu.VMEM(frag, bf16),
            pltpu.VMEM((TOK, 128), f32),
            dma((8,)), dma((NX,)), dma((NX,)), dma((2,)), dma((NY,)), dma((4,)), dma((4,)), dma((2,)), dma((NY,)),
            dma((NX,)), dma((NX,)), dma((NX,)), dma((NX,)), dma((NX,)),
            dma((NX,)), dma((NX,)), dma((4,)), dma((2,)), dma, dma,
        ],
        compiler_params=pltpu.CompilerParams(
            collective_id=bit, has_side_effects=True, vmem_limit_bytes=56 * 1024 * 1024
        ),
        cost_estimate=pl.CostEstimate(flops=2 * 10**9, bytes_accessed=6 * 10**6, transcendentals=128),
    )
    exponent = lax.dynamic_index_in_dim(gossip_exponent, fragment_index[0], 0, keepdims=False)
    outs = lax.switch(
        exponent, [build(bit) for bit in range(BITS)],
        fragment_index, token_ids.reshape(1, TOK), layer_input, norm_gain.reshape(1, NX * DF),
        value_weight.reshape(4, KV, KV), value_cotangent, anchor_weight[0], outer_momentum[0],
    )
    outs = pl.pallas_call(
        write_out,
        out_shape=shapes,
        in_specs=[vmem] * 6,
        out_specs=[anywhere] * 6,
        scratch_shapes=[dma((6,))],
    )(*outs)
    value, back, grad, new_anchor, new_momentum, merged = outs
    return value, back, grad[None], new_anchor[None], new_momentum[None], merged[None]


def solution(mesh):
    tokens = ("replica", "fsdp")
    whole = P("replica", "fsdp", "tensor")
    return jax.shard_map(
        local,
        mesh=mesh,
        in_specs=(P(tokens, None), P(), whole, P(tokens, "tensor"), P(tokens), whole, whole, P(), P()),
        out_specs=(P(tokens, "tensor"), P(tokens, "tensor"), whole, whole, whole, whole),
        check_vma=False,
    )
```

time: 104 us -> 95.8 us (0.921)
  the two profiles are of different devices: /device:TPU:1 before, /device:TPU:10 now
where the time goes in v3:
time: 95.8 us; the launch traced here: 95.6 us
  Pallas kernels  92.4 us (96%)
  between operations  1.94 us (2%)
  local copies, waits for them, and re-layouts  1.24 us (1%)
    pallas_call x1, Pallas kernels, local(): lax.switch(exponent, [build(bit) for bit in range(BITS)], fragment_index,...  91.2 us

profile of v3, /device:TPU:10, one launch (start us, length us, event | category | flops | bytes accessed | tf_op | source)
XLA Modules:
  0.0 95.6 jit_solution(10975372644909671408)
XLA Ops:
  1.3 1.2 %dynamic_slice.4 = s32[1]{0:T(128)} dynamic-slice(s32[4]{0:T(128)} %param.21, s32[]{:T(128)S(6)} %select_n.4), dynamic_slice_sizes={1} | dynamic-slice | bytes 12 | tf_op jit(solution)/shard_map/jit(dynamic_index_in_dim)/dynamic_slice | solution.py:430
  3.2 91.2 %conditional.1 = ((bf16[128,256]{1,0:T(8,128)(2,1)S(1)}, bf16[128,2048]{1,0:T(8,128)(2,1)S(1)}, bf16[1024,256]{1,0:T(8,128)(2,1)S(1)}, f32[256,256]{1,0:T(8,128)...) conditional(s32[]{:T(128)} %bitcast.1, (s32[1]{0:T(128)}, ...), branch_computations={%region_0.1_spmd, %region_1.2_spmd, %region_2.3_spmd, %region_3.4_... | conditional | flops 2000000000 | bytes 6000008 | solution.py:431
  3.2 91.2 %branch_0_fun.1 = (bf16[128,256]{1,0:T(8,128)(2,1)S(1)}, bf16[128,2048]{1,0:T(8,128)(2,1)S(1)}, bf16[1024,256]{1,0:T(8,128)(2,1)S(1)}, f32[256,256]{1,0:T(8,128)...) custom-call(s32[1]{0:T(128)} %get-tuple-element.80.frag_ref, s32[1,128]{1,0:T(1,128)} %get-tuple-element.81.ids_hbm, ...), custom_call_target="tpu_custom_call" | custom-call | flops 2000000000 | bytes 6000000 | tf_op jit(solution)/shard_map/cond/branch_0_fun/pallas_call | solution.py:431
  94.4 1.2 %shard_map.136 = (bf16[128,256]{1,0:T(8,128)(2,1)}, bf16[128,2048]{1,0:T(8,128)(2,1)}, bf16[1024,256]{1,0:T(8,128)(2,1)}, f32[256,256]{1,0:T(8,128)}, f32[256,256]{1,0:T(8,128)}, /*index=5*/bf16[256,256]{1,0:T(8,128)(2,1)}) custom-call(bf16[128,256]{1,0:T(8,128)(2,1)S(1)} %get-tuple-element.138.refs_0_, bf16[128,2048]{1,0:T(8,128)(2,1)S(1)} %get-tuple-element.139.refs_1_, ...), custom_call_target="tpu_custom_call" | custom-call | tf_op jit(solution)/shard_map/pallas_call | solution.py:436
